TPU v7x, 128 devices: a whole 4x4x4 slice. The times are simulated.
128 devices in a mesh: depth: 2 (over core), row: 4 (over x), col: 16 (over z, y).
Axes of the slice: x: 4, y: 4, z: 4, core: 2. Of those that a mesh axis runs over, the one named last changes fastest.
Arguments:
- tokens: bfloat16 [512, 6144], P(('depth', 'col'), 'row'), may hold values from -6 to 6
- up_weight: bfloat16 [6144, 24576], P('row', ('col', 'depth')), may hold values from -0.109375 to 0.109375
- down_weight: bfloat16 [24576, 6144], P(('col', 'depth'), 'row'), may hold values from -0.0546875 to 0.0546875
- grad_out: bfloat16 [512, 6144], P(('depth', 'col'), 'row'), may hold values from -6 to 6
- block_mask: int32 [2, 96, 24], replicated, may hold values 0 or 1
Outputs:
- out: bfloat16 [512, 6144], P(('depth', 'col'), 'row')
- grad_tokens: bfloat16 [512, 6144], P(('depth', 'col'), 'row')
- grad_up: bfloat16 [6144, 24576], P('row', ('col', 'depth'))
- grad_down: bfloat16 [24576, 6144], P(('col', 'depth'), 'row')
All inputs are finite; a program needn't handle non-finite values.
Results may differ from a plain program's by a relative error of at most 0.03.
Values may be sent and summed in bfloat16 or wider, within the bound.
A program may use at most 128 MiB of HBM per device.

v0:
```python
import jax
import jax.numpy as jnp
from jax import lax
from jax.sharding import PartitionSpec as P

BLOCK = 256


gelu_scale = 0.7978845608028654
gelu_cubic = 0.044715


def gelu_value(pre):
    inner = gelu_scale * (pre + gelu_cubic * pre * pre * pre)
    return 0.5 * pre * (1.0 + jnp.tanh(inner))


def gelu_slope(pre):
    inner = gelu_scale * (pre + gelu_cubic * pre * pre * pre)
    bend = jnp.tanh(inner)
    return 0.5 * (1.0 + bend) + 0.5 * pre * (1.0 - bend * bend) * gelu_scale * (
        1.0 + 3.0 * gelu_cubic * pre * pre
    )


def spread_blocks(picked, block):
    outer, inner = picked.shape
    spread = jnp.broadcast_to(picked[:, None, :, None], (outer, block, inner, block))
    return spread.reshape(outer * block, inner * block).astype(jnp.bfloat16)


def times_transposed(left, right):
    return lax.dot_general(
        left, right, (((1,), (1,)), ((), ())), preferred_element_type=jnp.float32
    )


def over_rows(left, right):
    return lax.dot_general(
        left, right, (((0,), (0,)), ((), ())), preferred_element_type=jnp.float32
    )


def grouped_rows(left, right, groups):
    width = left.shape[1] // groups
    left_parts = left.reshape(left.shape[0], groups, width)
    right_parts = right.reshape(groups, width, right.shape[1])
    partial_value = jnp.einsum(
        "rpw,pwc->prc", left_parts, right_parts, preferred_element_type=jnp.float32
    )
    return jnp.sum(partial_value.astype(jnp.bfloat16).astype(jnp.float32), axis=0)


def grouped_transposed(left, right, groups):
    width = left.shape[1] // groups
    left_parts = left.reshape(left.shape[0], groups, width)
    right_parts = right.reshape(right.shape[0], groups, width)
    partial_value = jnp.einsum(
        "rpw,cpw->prc", left_parts, right_parts, preferred_element_type=jnp.float32
    )
    return jnp.sum(partial_value.astype(jnp.bfloat16).astype(jnp.float32), axis=0)


def body(tokens, up_weight, down_weight, grad_out, block_mask):
    row_index = lax.axis_index("row")
    col_index = lax.axis_index("col")
    depth_index = lax.axis_index("depth")
    depths = lax.axis_size("depth")
    feature_tile = up_weight.shape[0]
    hidden_slice = up_weight.shape[1]
    feature_blocks = feature_tile // BLOCK
    up_tile = lax.all_gather(up_weight, "depth", axis=1, tiled=True)
    down_tile = lax.all_gather(down_weight, "depth", axis=0, tiled=True)
    hidden_blocks = up_tile.shape[1] // BLOCK
    corner = (col_index * hidden_blocks, row_index * feature_blocks)
    picked_up = lax.dynamic_slice(block_mask[0], corner, (hidden_blocks, feature_blocks))
    picked_down = lax.dynamic_slice(block_mask[1], corner, (hidden_blocks, feature_blocks))
    up_mask = spread_blocks(picked_up.T, BLOCK)
    down_mask = spread_blocks(picked_down, BLOCK)
    up_used = up_tile * up_mask
    down_used = down_tile * down_mask
    features = lax.all_gather(tokens, "col", axis=0, tiled=True)
    pre_held = lax.psum_scatter(
        jnp.dot(features, up_used, preferred_element_type=jnp.float32).astype(jnp.bfloat16),
        "row",
        scatter_dimension=0,
        tiled=True,
    ).astype(jnp.float32)
    act_all = lax.all_gather(gelu_value(pre_held).astype(jnp.bfloat16), "row", axis=0, tiled=True)
    out = lax.psum_scatter(
        grouped_rows(act_all, down_used, depths).astype(jnp.bfloat16),
        "col",
        scatter_dimension=0,
        tiled=True,
    )
    act_columns = lax.all_to_all(act_all, "depth", split_axis=1, concat_axis=0, tiled=True)
    grad_features = lax.all_gather(grad_out, "col", axis=0, tiled=True)
    grad_act_held = lax.psum_scatter(
        times_transposed(grad_features, down_used).astype(jnp.bfloat16),
        "row",
        scatter_dimension=0,
        tiled=True,
    ).astype(jnp.float32)
    grad_pre_held = (grad_act_held * gelu_slope(pre_held)).astype(jnp.bfloat16)
    grad_pre_all = lax.all_gather(grad_pre_held, "row", axis=0, tiled=True)
    grad_tokens = lax.psum_scatter(
        grouped_transposed(grad_pre_all, up_used, depths).astype(jnp.bfloat16),
        "col",
        scatter_dimension=0,
        tiled=True,
    )
    grad_columns = lax.all_to_all(grad_pre_all, "depth", split_axis=1, concat_axis=0, tiled=True)
    down_sum = over_rows(act_columns, lax.all_gather(grad_features, "depth", axis=0, tiled=True))
    up_sum = over_rows(lax.all_gather(features, "depth", axis=0, tiled=True), grad_columns)
    up_share_mask = lax.dynamic_slice_in_dim(up_mask, depth_index * hidden_slice, hidden_slice, 1)
    down_share_mask = lax.dynamic_slice_in_dim(
        down_mask, depth_index * hidden_slice, hidden_slice, 0
    )
    grad_up = (up_sum * up_share_mask).astype(jnp.bfloat16)
    grad_down = (down_sum * down_share_mask).astype(jnp.bfloat16)
    return (out, grad_tokens, grad_up, grad_down)


def solution(mesh):
    in_specs = (
        P(("depth", "col"), "row"),
        P("row", ("col", "depth")),
        P(("col", "depth"), "row"),
        P(("depth", "col"), "row"),
        P(),
    )
    out_specs = (
        P(("depth", "col"), "row"),
        P(("depth", "col"), "row"),
        P("row", ("col", "depth")),
        P(("col", "depth"), "row"),
    )
    return jax.shard_map(body, mesh=mesh, in_specs=in_specs, out_specs=out_specs, check_vma=False)
```

profile of v0, /device:TPU:1, one launch (start us, length us, event | category | flops | bytes accessed | tf_op | source)
XLA Modules:
  0.0 300.1 jit_solution(14748905837770523841)
XLA Ops:
  7.2 0.7 all-gather.5.cloned.1.call-update
  8.0 0.7 all-gather.7.cloned.1.call-update
  9.5 4.2 %copy.74 = bf16[192,8,6,256]{3,1,2,0:T(8,128)(2,1)} copy(bf16[192,8,6,256]{3,2,1,0:T(8,128)(2,1)S(1)} %bitcast.50) | data formatting | bytes 9437184
  13.7 21.5 %all_gather.25 = bf16[256,1536]{1,0:T(8,128)(2,1)S(1)} all-gather(bf16[16,1536]{1,0:T(8,128)(2,1)S(1)} %copy-done.4), channel_id=1, replica_groups=mesh['depth'=2,'row'=4,'col'=16] {'col'}, dimensions={0}, use_global_device_ids=true | all-gather | bytes 835584 | tf_op jit(solution)/shard_map/all_gather | solution.py:82
  35.2 5.3 %mul.74 = bf16[1536,1536]{1,0:T(8,128)(2,1)S(1)} multiply(bf16[1536,1536]{1,0:T(8,128)(2,1)} %all-gather.5.cloned.1.call-done, bf16[1536,1536]{1,0:T(8,128)(2,1)} %bitcast.48) | non-fusion elementwise | flops 2359296 | bytes 14155776 | tf_op jit(solution)/shard_map/mul | solution.py:80
  40.6 2.2 copy-done
  42.8 1.4 fusion.7
  44.3 1.2 copy.64
  46.1 4.2 %copy.75 = bf16[192,8,6,256]{3,1,2,0:T(8,128)(2,1)} copy(bf16[192,8,6,256]{3,2,1,0:T(8,128)(2,1)S(1)} %bitcast.51) | data formatting | bytes 9437184
  50.3 18.7 %all_gather.28 = bf16[256,1536]{1,0:T(8,128)(2,1)S(1)} all-gather(bf16[16,1536]{1,0:T(8,128)(2,1)S(1)} %copy-done.5), channel_id=1, replica_groups=mesh['depth'=2,'row'=4,'col'=16] {'col'}, dimensions={0}, use_global_device_ids=true | all-gather | bytes 835584 | tf_op jit(solution)/shard_map/all_gather | solution.py:97
  69.0 5.4 %mul.81 = bf16[1536,1536]{1,0:T(8,128)(2,1)S(1)} multiply(bf16[1536,1536]{1,0:T(8,128)(2,1)} %all-gather.7.cloned.1.call-done, bf16[1536,1536]{1,0:T(8,128)(2,1)} %bitcast.52) | non-fusion elementwise | flops 2359296 | bytes 14155776 | tf_op jit(solution)/shard_map/mul | solution.py:81
  74.5 2.1 copy-done.1
  76.6 1.4 fusion.8
  78.0 1.2 copy.66
  80.4 30.4 %reduce-scatter.15.cloned.1.call-done = bf16[64,1536]{1,0:T(8,128)(2,1)} async-done(((bf16[256,1536]{1,0:T(8,128)(2,1)}), bf16[64,1536]{1,0:T(8,128)(2,1)}) %reduce-scatter.15.cloned.1.call-update) | async-done | bytes 196624 | tf_op jit(solution)/shard_map/reduce_scatter | solution.py:98
  110.8 1.3 fusion.20
  112.1 10.9 %all_gather.29 = bf16[256,1536]{1,0:T(8,128)(2,1)S(1)} all-gather(bf16[64,1536]{1,0:T(8,128)(2,1)S(1)} %get-tuple-element.24), channel_id=1, replica_groups=mesh['depth'=2,'row'=4,'col'=16] {'row'}, dimensions={0}, use_global_device_ids=true | all-gather | bytes 983040 | tf_op jit(solution)/shard_map/all_gather | solution.py:105
  123.0 1.2 copy.55
  124.1 5.2 %fusion.10 = bf16[256,1536]{1,0:T(8,128)(2,1)} fusion(bf16[256,2,768]{0,2,1:T(8,128)(2,1)} %bitcast.7, bf16[192,2,8,768]{3,2,1,0:T(8,128)(2,1)} %bitcast.54), kind=kOutput, calls=%fused_computation.13 | convolution fusion | flops 1209139200 | bytes 6291456 | tf_op jit(solution)/shard_map/rpw,cpw->prc/dot_general | solution.py:58
  129.4 11.6 %all_gather.26 = bf16[256,1536]{1,0:T(8,128)(2,1)S(1)} all-gather(bf16[64,1536]{1,0:T(8,128)(2,1)S(1)} %get-tuple-element.25), channel_id=1, replica_groups=mesh['depth'=2,'row'=4,'col'=16] {'row'}, dimensions={0}, use_global_device_ids=true | all-gather | bytes 983040 | tf_op jit(solution)/shard_map/all_gather | solution.py:89
  141.2 4.8 %fusion.9 = bf16[256,1536]{1,0:T(8,128)(2,1)} fusion(bf16[256,2,768]{0,2,1:T(8,128)(2,1)S(1)} %bitcast.56, bf16[2,768,1536]{2,1,0:T(8,128)(2,1)} %bitcast.55), kind=kOutput, calls=%fused_computation.12 | convolution fusion | flops 1209139200 | bytes 6291456 | tf_op jit(solution)/shard_map/rpw,pwc->prc/dot_general | solution.py:48
  146.0 1.8 constant_dynamic-slice_fusion
  147.9 2.4 copy.72
  150.3 11.4 %all_to_all.32 = bf16[256,2,768]{0,2,1:T(8,128)(2,1)S(1)} all-to-all(bf16[256,2,768]{0,2,1:T(8,128)(2,1)S(1)} %bitcast.57), channel_id=1, replica_groups=mesh['depth'=2,'row'=4,'col'=16] {'depth'}, dimensions={1} | all-to-all | bytes 1572864 | tf_op jit(solution)/shard_map/all_to_all | solution.py:96
  161.7 3.9 %all-to-all-start = ((bf16[256,2,768]{0,2,1:T(8,128)(2,1)}), bf16[256,2,768]{0,2,1:T(8,128)(2,1)S(1)}, u32[]{:S(2)}, u32[]{:S(2)}) async-start(bf16[256,2,768]{0,2,1:T(8,128)(2,1)} %bitcast.7), calls=%async_computation.2 | async-start | bytes 1572864 | tf_op jit(solution)/shard_map/all_to_all | solution.py:112
  165.9 1.3 all-to-all-done
  167.2 1.2 copy.58
  168.3 3.8 %fusion.3 = bf16[1536,768]{0,1:T(8,128)(2,1)S(1)} fusion(bf16[1536,768]{0,1:T(8,128)(2,1)} %copy.72, bf16[512,768]{1,0:T(8,128)(2,1)} %bitcast.61, bf16[512,1536]{1,0:T(8,128)(2,1)} %all-gather.9.cloned.1.call-done), kind=kOutput, calls=%fused_computation.4 | convolution fusion | flops 1211498496 | bytes 7077888 | tf_op jit(solution)/shard_map/dot_general | solution.py:39
  172.2 2.4 copy.61
  174.6 5.0 %multiply_convert_fusion = bf16[768,1536]{1,0:T(8,128)(2,1)} fusion(bf16[512,768]{1,0:T(8,128)(2,1)S(1)} %bitcast.60, bf16[512,1536]{1,0:T(8,128)(2,1)} %all-gather.11.cloned.1.call-done, bf16[1536,1536]{1,0:T(8,128)(2,1)} %bitcast.53, s32[]{:T(128)S(6)} %select_n.14), kind=kOutput, calls=%fused_computation.5 | convolution fusion | flops 1211498496 | bytes 7077892 | tf_op jit(solution)/shard_map/dot_general | solution.py:39
  179.6 37.9 %reduce-scatter.11.cloned.1.call-done = bf16[16,1536]{1,0:T(8,128)(2,1)} async-done(((bf16[256,1536]{1,0:T(8,128)(2,1)}), bf16[16,1536]{1,0:T(8,128)(2,1)}) %reduce-scatter.11.cloned.1.call-update) | async-done | bytes 49168 | tf_op jit(solution)/shard_map/reduce_scatter | solution.py:106
  217.5 75.7 %reduce-scatter.9.cloned.1.call-done = bf16[16,1536]{1,0:T(8,128)(2,1)} async-done(((bf16[256,1536]{1,0:T(8,128)(2,1)}), bf16[16,1536]{1,0:T(8,128)(2,1)}) %reduce-scatter.9.cloned.1.call-update) | async-done | bytes 49168 | tf_op jit(solution)/shard_map/reduce_scatter | solution.py:90
  (42 shorter events, 3.4 us)
Async XLA Ops:
  7.2 1.6 copy-start.6
  7.2 28.1 %all-gather.5.cloned.1.call-start = ((), (), s32[]{:S(2)}) async-start(), calls=%async_computation.6 | async-start | bytes 7077888 | tf_op jit(solution)/shard_map/all_gather | solution.py:72
  7.9 61.1 %all-gather.7.cloned.1.call-start = ((), (), s32[]{:S(2)}) async-start(), calls=%async_computation.7 | async-start | bytes 7077888 | tf_op jit(solution)/shard_map/all_gather | solution.py:73
  8.7 71.8 %reduce-scatter.13.cloned.1.call-start = ((), (), s32[]{:S(2)}) async-start(), calls=%async_computation.12 | async-start | bytes 983040 | tf_op jit(solution)/shard_map/reduce_scatter | solution.py:83
  9.5 4.2 %copy-start.4 = (bf16[16,1536]{1,0:T(8,128)(2,1)S(1)}, bf16[16,1536]{1,0:T(8,128)(2,1)}, u32[]{:S(2)}) copy-start(bf16[16,1536]{1,0:T(8,128)(2,1)} %param.5) | copy-start | bytes 147460
  35.2 5.4 %copy-start.2 = (bf16[256,1536]{1,0:T(8,128)(2,1)}, bf16[256,1536]{1,0:T(8,128)(2,1)S(1)}, u32[]{:S(2)}) copy-start(bf16[256,1536]{1,0:T(8,128)(2,1)S(1)} %all_gather.25) | copy-start | bytes 2359300
  40.6 2.3 copy-start
  45.4 65.4 %reduce-scatter.15.cloned.1.call-start = ((), (), s32[]{:S(2)}) async-start(), calls=%async_computation.13 | async-start | bytes 983040 | tf_op jit(solution)/shard_map/reduce_scatter | solution.py:98
  46.1 4.2 %copy-start.5 = (bf16[16,1536]{1,0:T(8,128)(2,1)S(1)}, bf16[16,1536]{1,0:T(8,128)(2,1)}, u32[]{:S(2)}) copy-start(bf16[16,1536]{1,0:T(8,128)(2,1)} %param.8) | copy-start | bytes 147460
  69.0 5.4 %copy-start.3 = (bf16[256,1536]{1,0:T(8,128)(2,1)}, bf16[256,1536]{1,0:T(8,128)(2,1)S(1)}, u32[]{:S(2)}) copy-start(bf16[256,1536]{1,0:T(8,128)(2,1)S(1)} %all_gather.28) | copy-start | bytes 2359300
  74.4 2.1 copy-start.1
  79.2 89.2 %all-gather.9.cloned.1.call-start = ((), (), s32[]{:S(2)}) async-start(), calls=%async_computation.10 | async-start | bytes 2359296 | tf_op jit(solution)/shard_map/all_gather | solution.py:114
  79.8 94.8 %all-gather.11.cloned.1.call-start = ((), (), s32[]{:S(2)}) async-start(), calls=%async_computation.11 | async-start | bytes 2359296 | tf_op jit(solution)/shard_map/all_gather | solution.py:113
  80.3 137.2 %reduce-scatter.11.cloned.1.call-start = ((), (), s32[]{:S(2)}) async-start(), calls=%async_computation.9 | async-start | bytes 835584 | tf_op jit(solution)/shard_map/reduce_scatter | solution.py:106
  129.3 163.9 %reduce-scatter.9.cloned.1.call-start = ((), (), s32[]{:S(2)}) async-start(), calls=%async_computation.8 | async-start | bytes 835584 | tf_op jit(solution)/shard_map/reduce_scatter | solution.py:90
  161.7 5.5 %all-to-all-start = ((bf16[256,2,768]{0,2,1:T(8,128)(2,1)}), bf16[256,2,768]{0,2,1:T(8,128)(2,1)S(1)}, u32[]{:S(2)}, u32[]{:S(2)}) async-start(bf16[256,2,768]{0,2,1:T(8,128)(2,1)} %bitcast.7), calls=%async_computation.2 | async-start | bytes 1572864 | tf_op jit(solution)/shard_map/all_to_all | solution.py:112
Sparse Core Ops, SparseCore 0:
  9.7 20.7 all-gather.4
  32.1 18.4 all-gather.6
  53.6 22.2 reduce-scatter.12
  79.3 31.4 reduce-scatter.14
  112.3 13.7 all-gather.8
  127.6 13.8 all-gather.10
  145.2 72.2 reduce-scatter.10
  221.3 71.9 reduce-scatter.8
where the time goes:
time: 301 us; the launch traced here: 300 us
  waiting for transfers between devices  148 us (49%)
  blocking collectives  74 us (25%)
  local copies, waits for them, and re-layouts  26 us (9%)
  matrix products  21.6 us (7%)
  between operations  14.3 us (5%)
  other arithmetic  12 us (4%)
  starting transfers between devices  4.21 us (1%)
    reduce_scatter x1, waiting for transfers between devices, body(): lax.psum_scatter(grouped_rows(act_all, down_used, depths).astype(jnp.bflo...  75.7 us
    reduce_scatter x1, waiting for transfers between devices, body(): lax.psum_scatter(grouped_transposed(grad_pre_all, up_used, depths).astype...  37.9 us
    reduce_scatter x1, waiting for transfers between devices, body(): lax.psum_scatter(times_transposed(grad_features, down_used).astype(jnp.bf...  30.4 us
    all_gather x1, blocking collectives, body(): features = lax.all_gather(tokens, 'col', axis=0, tiled=True)  21.5 us
    unnamed x22, local copies, waits for them, and re-layouts  20.1 us
    all_gather x1, blocking collectives, body(): grad_features = lax.all_gather(grad_out, 'col', axis=0, tiled=True)  18.7 us
    all_gather x1, blocking collectives, body(): lax.all_gather(gelu_value(pre_held).astype(jnp.bfloat16), 'row', axis=0,...  11.6 us
    all_to_all x1, blocking collectives, body(): lax.all_to_all(act_all, 'depth', split_axis=1, concat_axis=0, tiled=True)  11.4 us
  transfers between devices with their start and end apart: 9, of which 4 were waited for; matrix products, arithmetic and copies ran while one was open for 18% of the time, Pallas kernels for 0%

commit v1 on v0

v1 whole, which is shorter than its diff:
```python
import jax
import jax.numpy as jnp
from jax import lax
from jax.experimental import pallas as pl
from jax.experimental.pallas import tpu as pltpu
from jax.sharding import PartitionSpec as P

BLOCK = 256
RING = 4
MESH = pl.DeviceIdType.MESH

gelu_scale = 0.7978845608028654
gelu_cubic = 0.044715

SCHEDULE = (
    [("mm", 0, 0), ("pass", 0), ("pass", 1), ("mm", 0, 3), ("comb", 0, 0), ("mm", 0, 1), ("comb", 0, 3)]
    + [("last", 0), ("last", 1), ("mm", 0, 2), ("comb", 0, 1), ("fin", 0, 0)]
    + [("mm", 1, 2), ("comb", 0, 2), ("fin", 0, 3)]
    + [("mm", 1, 1), ("comb", 1, 2), ("fin", 0, 1), ("fin", 0, 2)]
    + [("mm", 1, 3), ("comb", 1, 1), ("agf", 0, 0)]
    + [("mm", 1, 0), ("comb", 1, 3), ("fin", 1, 2), ("agf", 0, 3), ("agf", 0, 1)]
    + [("comb", 1, 0), ("fin", 1, 1), ("agf", 0, 2), ("om", 0, 0), ("fin", 1, 3), ("om", 0, 3)]
    + [("fin", 1, 0), ("agf", 1, 2), ("agf", 1, 1), ("om", 0, 1), ("zs", 0, 0), ("zs", 0, 3), ("om", 0, 2)]
    + [("agf", 1, 3), ("agf", 1, 0), ("zs", 0, 1), ("zs", 0, 2)]
    + [("om", 1, 2), ("zc", 0), ("om", 1, 1), ("zs", 1, 2), ("zf", 0), ("om", 1, 3), ("zs", 1, 1)]
    + [("om", 1, 0), ("zs", 1, 3), ("zc", 1), ("zs", 1, 0), ("yf", 0), ("tt",), ("at",), ("gdn",)]
    + [("zf", 1), ("gup",), ("yf", 1)]
)


def gelu_pair(pre):
    inner = gelu_scale * (pre + gelu_cubic * pre * pre * pre)
    bend = jnp.tanh(inner)
    value = 0.5 * pre * (1.0 + bend)
    slope = 0.5 * (1.0 + bend) + 0.5 * pre * (1.0 - bend * bend) * gelu_scale * (
        1.0 + 3.0 * gelu_cubic * pre * pre
    )
    return value, slope


def kernel(
    tok_h, up_h, down_h, gout_h, mask_h,
    out_h, gtok_h, gup_h, gdown_h,
    feats, wu, wd, masks, part, own_part, relay, comb_out, comb_in, slopes, hidden,
    pair_out, pair_in, kept, zsend, zrelay, zown, zcomb_out, zcomb_in, fsend, fown, frecv,
    small, tok_t, act_t, gup_v, gdown_v,
    send_sem, recv_sem, local_sem,
):
    f32, bf16 = jnp.float32, jnp.bfloat16
    width = wu.shape[0]
    hid = wu.shape[1]
    x = lax.axis_index("row")
    col = lax.axis_index("col")
    d = lax.axis_index("depth")
    z, y = lax.div(col, RING), lax.rem(col, RING)
    other = 1 - d
    major, minor = (z, y), (y, z)

    def turn(value, by):
        return lax.rem(value + by, RING)

    def major_peer(s, by):
        return {"col": turn(z, by) * RING + y} if s == 0 else {"col": z * RING + turn(y, by)}

    def minor_peer(s, by):
        return major_peer(1 - s, by)

    def row_peer(by):
        return {"row": turn(x, by)}

    sibling = {"depth": other}
    numbers = {}

    def remote(name, src, dst, peer):
        n = numbers.setdefault(name, len(numbers))
        return pltpu.make_async_remote_copy(
            src_ref=src, dst_ref=dst, send_sem=send_sem.at[n], recv_sem=recv_sem.at[n],
            device_id=peer, device_id_type=MESH,
        )

    sent = []

    def send(name, src, dst, peer):
        copy = remote(name, src, dst, peer)
        copy.start()
        sent.append(copy)

    def arrived(name, dst):
        remote(name, dst, dst, sibling).wait_recv()

    sources = (tok_h, gout_h)
    loads = [
        pltpu.make_async_copy(sources[0], feats.at[0, z, y, d], local_sem.at[0]),
        pltpu.make_async_copy(sources[1], feats.at[1, y, z, d], local_sem.at[1]),
        pltpu.make_async_copy(up_h, wu, local_sem.at[2]),
        pltpu.make_async_copy(mask_h, masks, local_sem.at[4]),
        pltpu.make_async_copy(down_h, wd, local_sem.at[3]),
    ]
    for load in loads:
        load.start()

    peers = [row_peer(1), row_peer(3), sibling]
    for by in (1, 2, 3):
        peers += [minor_peer(0, by), minor_peer(1, by)]
    barrier = pltpu.get_barrier_semaphore()
    for peer in peers:
        pl.semaphore_signal(barrier, inc=1, device_id=peer, device_id_type=MESH)
    pl.semaphore_wait(barrier, len(peers))

    hidden_corner = (col * 2 + d) * (hid // BLOCK)
    feature_corner = x * (width // BLOCK)

    def mask_at(which, hb, fb):
        return masks[which, hidden_corner + hb, feature_corner + fb].astype(f32)

    for s in (0, 1):
        for by in (1, 3, 2):
            send(("g1", s, by), sources[s], feats.at[s, major[s], minor[s], d], minor_peer(s, by))
    loads[3].wait()
    loads[2].wait()
    for fb in range(width // BLOCK):
        for hb in range(hid // BLOCK):
            tile = (pl.ds(fb * BLOCK, BLOCK), pl.ds(hb * BLOCK, BLOCK))
            wu[tile] = wu[tile] * mask_at(0, hb, fb).astype(bf16)
    for s in (0, 1):
        loads[s].wait()
        for by in (1, 3, 2):
            arrived(("g1", s, by), feats.at[s, major[s], turn(minor[s], RING - by), d])
        mine = feats.at[s, major[s], :, d]
        send(("g2", s, 1), mine, mine, major_peer(s, 1))
        send(("g2", s, 3), mine, mine, major_peer(s, 3))
        send(("pair", s, 0), mine, mine, sibling)
    loads[4].wait()
    for fb in range(width // BLOCK):
        for hb in range(hid // BLOCK):
            tile = (pl.ds(hb * BLOCK, BLOCK), pl.ds(fb * BLOCK, BLOCK))
            wd[tile] = wd[tile] * mask_at(1, hb, fb).astype(bf16)

    def do_pass(s):
        for by, half in ((1, 0), (3, 2)):
            a = turn(major[s], RING - by)
            whole = feats.at[s, a, :, d]
            arrived(("g2", s, by), whole)
            part_of = feats.at[s, a, pl.ds(half, 2), d]
            send(("g3", s, by), part_of, part_of, major_peer(s, by))
            send(("pair", s, RING - by), whole, whole, sibling)

    def do_last(s):
        a = turn(major[s], 2)
        for by, half in ((1, 0), (3, 2)):
            part_of = feats.at[s, a, pl.ds(half, 2), d]
            arrived(("g3", s, by), part_of)
            send(("pair2", s, by), part_of, part_of, sibling)

    def places(s, k):
        a = turn(major[s], k)
        return a, turn(x + RING - a, 0)

    def product(s, left, tile):
        if s == 0:
            return jnp.dot(left, wu[:, tile], preferred_element_type=f32)
        return lax.dot_general(
            left, wd[tile, :], (((1,), (1,)), ((), ())), preferred_element_type=f32
        )

    def product_back(s, left, tile):
        if s == 0:
            return jnp.dot(left, wd[:, tile], preferred_element_type=f32)
        return lax.dot_general(
            left, wu[tile, :], (((1,), (1,)), ((), ())), preferred_element_type=f32
        )

    def do_mm(s, k):
        a, m = places(s, k)
        if k == 2:
            for by, half in ((1, 0), (3, 2)):
                arrived(("pair2", s, by), feats.at[s, a, pl.ds(half, 2), other])
        else:
            arrived(("pair", s, k), feats.at[s, a, :, other])
        left = jnp.concatenate(
            [feats[s, a, turn(m, j)].reshape(32, width) for j in range(RING)], axis=0
        )
        for n in range(hid // BLOCK):
            tile = pl.ds(n * BLOCK, BLOCK)
            value = product(s, left, tile)
            part[s, k, :, :, tile] = value.astype(bf16).reshape(8, 16, BLOCK)
            own_part[s, k, :, :, tile] = value[:32].reshape(2, 16, BLOCK)
        send(("x1", s, k, 1), part.at[s, k, pl.ds(3, 2)], relay.at[s, 0, k], row_peer(1))
        send(("x1", s, k, 3), part.at[s, k, pl.ds(5, 2)], relay.at[s, 1, k], row_peer(3))

    def do_comb(s, k):
        for by, side, own, got in ((1, 0, 2, 1), (3, 1, 7, 0)):
            arrived(("x1", s, k, by), relay.at[s, side, k])
            total = part[s, k, own].astype(f32) + relay[s, side, k, got].astype(f32)
            comb_out[s, side, k] = total.astype(bf16)
            send(("x2", s, k, by), comb_out.at[s, side, k], comb_in.at[s, side, k], row_peer(by))

    def do_fin(s, k):
        a, m = places(s, k)
        for by, side in ((1, 0), (3, 1)):
            arrived(("x2", s, k, by), comb_in.at[s, side, k])
        for h in (0, 1):
            total = (
                own_part[s, k, h]
                + relay[s, 1 - h, k, 1 - h].astype(f32)
                + comb_in[s, h, k].astype(f32)
            )
            if s == 0:
                value, slope = gelu_pair(total)
                hidden[s, a, m, h] = value.astype(bf16)
                slopes[a, h] = slope
            else:
                hidden[s, a, m, h] = (total * slopes[m, h]).astype(bf16)
        block = hidden.at[s, a, m]
        for by in (1, 3):
            send(("a1", s, k, by), block, block, row_peer(by))

    def do_agf(s, k):
        a, m = places(s, k)
        for by, h in ((1, 0), (3, 1)):
            from_owner = turn(m, RING - by)
            arrived(("a1", s, k, by), hidden.at[s, a, from_owner])
            half = hidden.at[s, a, from_owner, h]
            send(("a2", s, k, by), half, half, row_peer(by))

    def do_om(s, k):
        a, m = places(s, k)
        for by, h in ((1, 0), (3, 1)):
            arrived(("a2", s, k, by), hidden.at[s, a, turn(m, 2), h])
        left = jnp.concatenate(
            [hidden[s, a, :, other].reshape(64, hid), hidden[s, a, :, d].reshape(64, hid)], axis=0
        )
        for n in range(width // BLOCK):
            tile = pl.ds(n * BLOCK, BLOCK)
            value = product_back(s, left, tile)
            pair_out[s, k, :, :, tile] = value[:64].astype(bf16).reshape(RING, 16, BLOCK)
            kept[s, k, :, :, tile] = value[64:].reshape(RING, 16, BLOCK)
        send(("p", s, k), pair_out.at[s, k], pair_in.at[s, k], sibling)

    def do_zs(s, k):
        arrived(("p", s, k), pair_in.at[s, k])
        total = kept[s, k] + pair_in[s, k].astype(f32)
        if k == 0:
            kept[s, k] = total
            return
        zsend[s, k] = total.astype(bf16)
        first, second = zsend.at[s, k, pl.ds(0, 2)], zsend.at[s, k, pl.ds(2, 2)]
        if k == 2:
            send(("z1", s, 1), first, zrelay.at[s, 0], major_peer(s, 1))
            send(("z1", s, 3), second, zrelay.at[s, 1], major_peer(s, 3))
        elif k == 1:
            send(("z0", s, 1), second, zown.at[s, 0], major_peer(s, 1))
        else:
            send(("z0", s, 3), first, zown.at[s, 1], major_peer(s, 3))

    def do_zc(s):
        for by, side, half in ((1, 0, 0), (3, 1, 2)):
            arrived(("z1", s, by), zrelay.at[s, side])
            total = zsend[s, by, pl.ds(half, 2)].astype(f32) + zrelay[s, side].astype(f32)
            zcomb_out[s, side] = total.astype(bf16)
            send(("z2", s, by), zcomb_out.at[s, side], zcomb_in.at[s, side], major_peer(s, by))

    def do_zf(s):
        for by, side in ((1, 0), (3, 1)):
            arrived(("z0", s, by), zown.at[s, side])
            arrived(("z2", s, by), zcomb_in.at[s, side])
        for h in (0, 1):
            rows = pl.ds(2 * h, 2)
            total = kept[s, 0, rows] + zown[s, 1 - h].astype(f32) + zcomb_in[s, h].astype(f32)
            fsend[s, rows] = total.astype(bf16)
            fown[s, rows] = total
        for by in (1, 3, 2):
            send(("f", s, by), fsend.at[s, turn(minor[s], by)], frecv.at[s, by - 1], minor_peer(s, by))

    stores = []

    def store(src, dst):
        copy = pltpu.make_async_copy(src, dst, local_sem.at[5 + len(stores)])
        copy.start()
        stores.append(copy)

    def do_yf(s):
        total = fown[s, minor[s]]
        for by in (1, 3, 2):
            arrived(("f", s, by), frecv.at[s, by - 1])
            total = total + frecv[s, by - 1].astype(f32)
        small[s] = total.astype(bf16)
        store(small.at[s], (out_h, gtok_h)[s])

    def do_tt():
        for a in range(RING):
            for n in range(width // BLOCK):
                tile = feats[0, a, :, :, :, pl.ds(n * BLOCK, BLOCK)].reshape(128, BLOCK)
                tok_t[pl.ds(n * BLOCK, BLOCK), pl.ds(a * 128, 128)] = tile.T

    def do_at():
        for a in range(RING):
            for n in range(hid // BLOCK):
                tile = hidden[0, a, :, :, :, pl.ds(n * BLOCK, BLOCK)].reshape(128, BLOCK)
                act_t[pl.ds(n * BLOCK, BLOCK), pl.ds(a * 128, 128)] = tile.T

    def swapped(ref, tile):
        return jnp.concatenate(
            [ref[1, b, a, :, :, tile].reshape(32, BLOCK) for a in range(RING) for b in range(RING)],
            axis=0,
        )

    def do_gdn():
        @pl.loop(0, width // BLOCK)
        def _(fb):
            tile = pl.ds(pl.multiple_of(fb * BLOCK, BLOCK), BLOCK)
            right = swapped(feats, tile)
            for hb in range(hid // BLOCK):
                rows = pl.ds(hb * BLOCK, BLOCK)
                value = jnp.dot(act_t[rows, :], right, preferred_element_type=f32)
                gdown_v[rows, tile] = (value * mask_at(1, hb, fb)).astype(bf16)

        store(gdown_v, gdown_h)

    def do_gup():
        for hb in range(hid // BLOCK):
            tile = pl.ds(hb * BLOCK, BLOCK)
            right = swapped(hidden, tile)

            @pl.loop(0, width // BLOCK)
            def _(fb):
                rows = pl.ds(pl.multiple_of(fb * BLOCK, BLOCK), BLOCK)
                value = jnp.dot(tok_t[rows, :], right, preferred_element_type=f32)
                gup_v[rows, tile] = (value * mask_at(0, hb, fb)).astype(bf16)

        store(gup_v, gup_h)

    steps = {
        "pass": do_pass, "last": do_last, "mm": do_mm, "comb": do_comb, "fin": do_fin, "agf": do_agf,
        "om": do_om, "zs": do_zs, "zc": do_zc, "zf": do_zf, "yf": do_yf,
        "tt": do_tt, "at": do_at, "gdn": do_gdn, "gup": do_gup,
    }
    for step in SCHEDULE:
        steps[step[0]](*step[1:])
    for copy in sent:
        copy.wait_send()
    for copy in stores:
        copy.wait()


def layer(tokens, up_weight, down_weight, grad_out, block_mask):
    rows, width = tokens.shape
    hid = up_weight.shape[1]
    bf16, f32 = jnp.bfloat16, jnp.float32
    V = pltpu.VMEM
    anywhere = pl.BlockSpec(memory_space=pl.ANY)
    return pl.pallas_call(
        kernel,
        out_shape=[
            jax.ShapeDtypeStruct((rows, width), bf16),
            jax.ShapeDtypeStruct((rows, width), bf16),
            jax.ShapeDtypeStruct((width, hid), bf16),
            jax.ShapeDtypeStruct((hid, width), bf16),
        ],
        in_specs=[anywhere] * 5,
        out_specs=[anywhere] * 4,
        scratch_shapes=[
            V((2, 4, 4, 2, 16, width), bf16),
            V((width, hid), bf16),
            V((hid, width), bf16),
            pltpu.SMEM(block_mask.shape, jnp.int32),
            V((2, 4, 8, 16, hid), bf16),
            V((2, 4, 2, 16, hid), f32),
            V((2, 2, 4, 2, 16, hid), bf16),
            V((2, 2, 4, 16, hid), bf16),
            V((2, 2, 4, 16, hid), bf16),
            V((4, 2, 16, hid), f32),
            V((2, 4, 4, 2, 16, hid), bf16),
            V((2, 4, 4, 16, width), bf16),
            V((2, 4, 4, 16, width), bf16),
            V((2, 4, 4, 16, width), f32),
            V((2, 4, 4, 16, width), bf16),
            V((2, 2, 2, 16, width), bf16),
            V((2, 2, 2, 16, width), bf16),
            V((2, 2, 2, 16, width), bf16),
            V((2, 2, 2, 16, width), bf16),
            V((2, 4, 16, width), bf16),
            V((2, 4, 16, width), f32),
            V((2, 3, 16, width), bf16),
            V((2, 16, width), bf16),
            V((width, 512), bf16),
            V((hid, 512), bf16),
            V((width, hid), bf16),
            V((hid, width), bf16),
            pltpu.SemaphoreType.DMA((120,)),
            pltpu.SemaphoreType.DMA((120,)),
            pltpu.SemaphoreType.DMA((9,)),
        ],
        compiler_params=pltpu.CompilerParams(
            collective_id=0, has_side_effects=True, vmem_limit_bytes=56 * 1024 * 1024
        ),
        cost_estimate=pl.CostEstimate(
            flops=12 * 512 * width * hid, bytes_accessed=8 * width * hid, transcendentals=0
        ),
    )(tokens, up_weight, down_weight, grad_out, block_mask)


def solution(mesh):
    in_specs = (
        P(("depth", "col"), "row"),
        P("row", ("col", "depth")),
        P(("col", "depth"), "row"),
        P(("depth", "col"), "row"),
        P(),
    )
    out_specs = (
        P(("depth", "col"), "row"),
        P(("depth", "col"), "row"),
        P("row", ("col", "depth")),
        P(("col", "depth"), "row"),
    )
    return jax.shard_map(layer, mesh=mesh, in_specs=in_specs, out_specs=out_specs, check_vma=False)
```

time: 301 us -> 83 us (0.28)
  waiting for transfers between devices: 148 us -> 0 us
  blocking collectives: 74 us -> 0 us
  Pallas kernels: 0 us -> 73 us
  matrix products: 21.6 us -> 0 us
  local copies, waits for them, and re-layouts: 26 us -> 9.09 us
  between operations: 14.3 us -> 0.64 us
  other arithmetic: 12 us -> 0 us
  starting transfers between devices: 4.21 us -> 0 us
    reduce_scatter x4 -> x0, waiting for transfers between devices: 144 us -> none  [the longest x1 75.7 us: body(): lax.psum_scatter(grouped_rows(act_all, down_used, depths).astype(jnp.bflo...]
    pallas_call x0 -> x1, Pallas kernels: none -> 73 us  [layer(): pl.pallas_call(kernel, out_shape=[jax.ShapeDtypeStruct((rows, width), bf1...]
    all_gather x4 -> x0, blocking collectives: 62.6 us -> none  [the longest x1 21.5 us: body(): features = lax.all_gather(tokens, 'col', axis=0, tiled=True)]
    dot_general x6 -> x0, matrix products: 21.6 us -> none  [the longest x2 8.79 us: over_rows(): lax.dot_general(left, right, (((0,), (0,)), ((), ())), preferred_element_...]
    all_to_all x1 -> x0, blocking collectives: 11.4 us -> none  [body(): lax.all_to_all(act_all, 'depth', split_axis=1, concat_axis=0, tiled=True)]
    unnamed x22 -> x7, local copies, waits for them, and re-layouts: 20.1 us -> 9.09 us
    mul x2 -> x0, other arithmetic: 10.7 us -> none  [the longest x1 5.39 us: body(): down_used = down_tile * down_mask]
    all_to_all x1 -> x0, starting transfers between devices: 3.9 us -> none  [body(): lax.all_to_all(grad_pre_all, 'depth', split_axis=1, concat_axis=0, tiled=...]
  transfers between devices with their start and end apart: 9 -> 0, of which waited for: 4 -> 0; matrix products, arithmetic and copies ran while one was open for 18% -> 0% of each run, Pallas kernels for 0% -> 0%
where the time goes in v1:
time: 83 us; the launch traced here: 82.7 us
  Pallas kernels  73 us (88%)
  local copies, waits for them, and re-layouts  9.09 us (11%)
    pallas_call x1, Pallas kernels, layer(): pl.pallas_call(kernel, out_shape=[jax.ShapeDtypeStruct((rows, width), bf1...  73 us
    unnamed x7, local copies, waits for them, and re-layouts  9.09 us

profile of v1, /device:TPU:1, one launch (start us, length us, event | category | flops | bytes accessed | tf_op | source)
XLA Modules:
  0.0 82.7 jit_solution(8959777088288103407)
XLA Ops:
  0.6 1.5 %copy.9.mask_h = s32[2,96,24]{2,1,0:T(8,128)} copy(s32[2,96,24]{1,2,0:T(8,128)} %param.9) | data formatting | bytes 36864 | tf_op args[4]
  2.1 73.0 %shard_map.84 = (bf16[16,1536]{1,0:T(8,128)(2,1)}, bf16[16,1536]{1,0:T(8,128)(2,1)}, bf16[1536,768]{1,0:T(8,128)(2,1)}, bf16[768,1536]{1,0:T(8,128)(2,1)}) custom-call(bf16[16,1536]{1,0:T(8,128)(2,1)} %tok_h.1, bf16[1536,768]{1,0:T(8,128)(2,1)} %up_h.1, bf16[768,1536]{1,0:T(8,128)(2,1)} %down_h.1, bf16[16,1536]{1,0:T(8,128)(2,1)} %gout_h.1, ...), custom_call_target="tpu_custom_call" | custom-call | flops 7247757312 | bytes 9437184 | tf_op jit(solution)/shard_map/pallas_call | solution.py:352
  75.1 1.4 %copy.14 = bf16[16,1536]{1,0:T(8,128)(2,1)} copy(bf16[16,1536]{1,0:T(8,128)(2,1)} %get-tuple-element.8) | data formatting | bytes 98304
  76.5 1.4 %copy.15 = bf16[16,1536]{1,0:T(8,128)(2,1)} copy(bf16[16,1536]{1,0:T(8,128)(2,1)} %get-tuple-element.9) | data formatting | bytes 98304
  77.9 0.0 copy-start
  77.9 3.4 %copy.16 = bf16[1536,768]{1,0:T(8,128)(2,1)} copy(bf16[1536,768]{1,0:T(8,128)(2,1)} %get-tuple-element.10) | data formatting | bytes 4718592
  81.3 0.0 copy-done
  81.3 1.4 %copy.17 = bf16[768,1536]{1,0:T(8,128)(2,1)} copy(bf16[768,1536]{1,0:T(8,128)(2,1)S(1)} %copy-done) | data formatting | bytes 4718592
Async XLA Ops:
  77.9 3.4 %copy-start = (bf16[768,1536]{1,0:T(8,128)(2,1)S(1)}, bf16[768,1536]{1,0:T(8,128)(2,1)}, u32[]{:S(2)}) copy-start(bf16[768,1536]{1,0:T(8,128)(2,1)} %get-tuple-element.11) | copy-start | bytes 7077892

commit v2 on v1

--- a/solution.py
+++ b/solution.py
@@ -13,18 +13,12 @@
 gelu_cubic = 0.044715
 
 SCHEDULE = (
-    [("mm", 0, 0), ("pass", 0), ("pass", 1), ("mm", 0, 3), ("comb", 0, 0), ("mm", 0, 1), ("comb", 0, 3)]
-    + [("last", 0), ("last", 1), ("mm", 0, 2), ("comb", 0, 1), ("fin", 0, 0)]
-    + [("mm", 1, 2), ("comb", 0, 2), ("fin", 0, 3)]
-    + [("mm", 1, 1), ("comb", 1, 2), ("fin", 0, 1), ("fin", 0, 2)]
-    + [("mm", 1, 3), ("comb", 1, 1), ("agf", 0, 0)]
-    + [("mm", 1, 0), ("comb", 1, 3), ("fin", 1, 2), ("agf", 0, 3), ("agf", 0, 1)]
-    + [("comb", 1, 0), ("fin", 1, 1), ("agf", 0, 2), ("om", 0, 0), ("fin", 1, 3), ("om", 0, 3)]
-    + [("fin", 1, 0), ("agf", 1, 2), ("agf", 1, 1), ("om", 0, 1), ("zs", 0, 0), ("zs", 0, 3), ("om", 0, 2)]
-    + [("agf", 1, 3), ("agf", 1, 0), ("zs", 0, 1), ("zs", 0, 2)]
-    + [("om", 1, 2), ("zc", 0), ("om", 1, 1), ("zs", 1, 2), ("zf", 0), ("om", 1, 3), ("zs", 1, 1)]
-    + [("om", 1, 0), ("zs", 1, 3), ("zc", 1), ("zs", 1, 0), ("yf", 0), ("tt",), ("at",), ("gdn",)]
-    + [("zf", 1), ("gup",), ("yf", 1)]
+    "own0", "own1", "mm00", "mm10", "comb00", "comb10", "pass0", "pass1", "fin00", "mm03", "mm01",
+    "mm13", "last0", "last1", "comb03", "mm02", "mm12", "tt", "comb13", "fin03", "comb01",
+    "comb02", "comb12", "mm11", "agf03", "fin02", "fin01", "fin12", "comb11", "om03", "agf02",
+    "fin13", "agf12", "zs03", "fin11", "agf01", "om02", "agf13", "fin10", "om12", "agf11", "zs02",
+    "om01", "zs12", "om13", "om11", "agf00", "zs01", "agf10", "zs13", "zc0", "zs11", "zc1", "om00",
+    "om10", "at", "gup0", "zs00", "gup1", "gup2", "zs10", "zf0", "zf1", "gdn", "yf0", "yf1",
 )
 
 
@@ -40,10 +34,10 @@
 
 def kernel(
     tok_h, up_h, down_h, gout_h, mask_h,
-    out_h, gtok_h, gup_h, gdown_h,
+    out_v, gtok_v, gup_v, gdown_v,
     feats, wu, wd, masks, part, own_part, relay, comb_out, comb_in, slopes, hidden,
     pair_out, pair_in, kept, zsend, zrelay, zown, zcomb_out, zcomb_in, fsend, fown, frecv,
-    small, tok_t, act_t, gup_v, gdown_v,
+    tok_t, act_t,
     send_sem, recv_sem, local_sem,
 ):
     f32, bf16 = jnp.float32, jnp.bfloat16
@@ -111,7 +105,7 @@
     feature_corner = x * (width // BLOCK)
 
     def mask_at(which, hb, fb):
-        return masks[which, hidden_corner + hb, feature_corner + fb].astype(f32)
+        return masks[which, feature_corner + fb, hidden_corner + hb].astype(f32)
 
     for s in (0, 1):
         for by in (1, 3, 2):
@@ -122,7 +116,12 @@
         for hb in range(hid // BLOCK):
             tile = (pl.ds(fb * BLOCK, BLOCK), pl.ds(hb * BLOCK, BLOCK))
             wu[tile] = wu[tile] * mask_at(0, hb, fb).astype(bf16)
-    for s in (0, 1):
+    loads[4].wait()
+    for fb in range(width // BLOCK):
+        for hb in range(hid // BLOCK):
+            tile = (pl.ds(hb * BLOCK, BLOCK), pl.ds(fb * BLOCK, BLOCK))
+            wd[tile] = wd[tile] * mask_at(1, hb, fb).astype(bf16)
+    def do_own(s):
         loads[s].wait()
         for by in (1, 3, 2):
             arrived(("g1", s, by), feats.at[s, major[s], turn(minor[s], RING - by), d])
@@ -130,12 +129,6 @@
         send(("g2", s, 1), mine, mine, major_peer(s, 1))
         send(("g2", s, 3), mine, mine, major_peer(s, 3))
         send(("pair", s, 0), mine, mine, sibling)
-    loads[4].wait()
-    for fb in range(width // BLOCK):
-        for hb in range(hid // BLOCK):
-            tile = (pl.ds(hb * BLOCK, BLOCK), pl.ds(fb * BLOCK, BLOCK))
-            wd[tile] = wd[tile] * mask_at(1, hb, fb).astype(bf16)
-
     def do_pass(s):
         for by, half in ((1, 0), (3, 2)):
             a = turn(major[s], RING - by)
@@ -272,20 +265,12 @@
         for by in (1, 3, 2):
             send(("f", s, by), fsend.at[s, turn(minor[s], by)], frecv.at[s, by - 1], minor_peer(s, by))
 
-    stores = []
-
-    def store(src, dst):
-        copy = pltpu.make_async_copy(src, dst, local_sem.at[5 + len(stores)])
-        copy.start()
-        stores.append(copy)
-
     def do_yf(s):
         total = fown[s, minor[s]]
         for by in (1, 3, 2):
             arrived(("f", s, by), frecv.at[s, by - 1])
             total = total + frecv[s, by - 1].astype(f32)
-        small[s] = total.astype(bf16)
-        store(small.at[s], (out_h, gtok_h)[s])
+        (out_v, gtok_v)[s][...] = total.astype(bf16)
 
     def do_tt():
         for a in range(RING):
@@ -315,31 +300,37 @@
                 value = jnp.dot(act_t[rows, :], right, preferred_element_type=f32)
                 gdown_v[rows, tile] = (value * mask_at(1, hb, fb)).astype(bf16)
 
-        store(gdown_v, gdown_h)
-
-    def do_gup():
-        for hb in range(hid // BLOCK):
-            tile = pl.ds(hb * BLOCK, BLOCK)
-            right = swapped(hidden, tile)
-
-            @pl.loop(0, width // BLOCK)
-            def _(fb):
-                rows = pl.ds(pl.multiple_of(fb * BLOCK, BLOCK), BLOCK)
-                value = jnp.dot(tok_t[rows, :], right, preferred_element_type=f32)
-                gup_v[rows, tile] = (value * mask_at(0, hb, fb)).astype(bf16)
-
-        store(gup_v, gup_h)
+    def do_gup(hb):
+        tile = pl.ds(hb * BLOCK, BLOCK)
+        right = swapped(hidden, tile)
+
+        for half in (0, 1):
+            rows = pl.ds(half * (width // 2), width // 2)
+            value = jnp.dot(tok_t[rows, :], right, preferred_element_type=f32)
+            for n in range(width // 2 // BLOCK):
+                fb = half * (width // 2 // BLOCK) + n
+                gup_v[pl.ds(fb * BLOCK, BLOCK), tile] = (
+                    value[n * BLOCK : (n + 1) * BLOCK] * mask_at(0, hb, fb)
+                ).astype(bf16)
 
     steps = {
-        "pass": do_pass, "last": do_last, "mm": do_mm, "comb": do_comb, "fin": do_fin, "agf": do_agf,
+        "own": do_own, "pass": do_pass, "last": do_last, "mm": do_mm, "comb": do_comb, "fin": do_fin, "agf": do_agf,
         "om": do_om, "zs": do_zs, "zc": do_zc, "zf": do_zf, "yf": do_yf,
         "tt": do_tt, "at": do_at, "gdn": do_gdn, "gup": do_gup,
     }
     for step in SCHEDULE:
-        steps[step[0]](*step[1:])
+        name = step.rstrip("0123")
+        steps[name](*[int(v) for v in step[len(name):]])
     for copy in sent:
         copy.wait_send()
-    for copy in stores:
+
+
+def write_out(*refs):
+    sources, targets, sems = refs[:4], refs[4:8], refs[8]
+    copies = [pltpu.make_async_copy(a, b, sems.at[i]) for i, (a, b) in enumerate(zip(sources, targets))]
+    for copy in copies:
+        copy.start()
+    for copy in copies:
         copy.wait()
 
 
@@ -349,16 +340,14 @@
     bf16, f32 = jnp.bfloat16, jnp.float32
     V = pltpu.VMEM
     anywhere = pl.BlockSpec(memory_space=pl.ANY)
-    return pl.pallas_call(
+    block_mask = jnp.transpose(block_mask, (0, 2, 1))
+    operands = (tokens, up_weight, down_weight, grad_out, block_mask)
+    shapes = ((rows, width), (rows, width), (width, hid), (hid, width))
+    results = pl.pallas_call(
         kernel,
-        out_shape=[
-            jax.ShapeDtypeStruct((rows, width), bf16),
-            jax.ShapeDtypeStruct((rows, width), bf16),
-            jax.ShapeDtypeStruct((width, hid), bf16),
-            jax.ShapeDtypeStruct((hid, width), bf16),
-        ],
-        in_specs=[anywhere] * 5,
-        out_specs=[anywhere] * 4,
+        out_shape=[V(shape, bf16) for shape in shapes],
+        in_specs=[pl.BlockSpec(memory_space=pltpu.HBM)] * 5,
+        out_specs=[pl.BlockSpec(memory_space=V)] * 4,
         scratch_shapes=[
             V((2, 4, 4, 2, 16, width), bf16),
             V((width, hid), bf16),
@@ -382,22 +371,27 @@
             V((2, 4, 16, width), bf16),
             V((2, 4, 16, width), f32),
             V((2, 3, 16, width), bf16),
-            V((2, 16, width), bf16),
             V((width, 512), bf16),
             V((hid, 512), bf16),
-            V((width, hid), bf16),
-            V((hid, width), bf16),
             pltpu.SemaphoreType.DMA((120,)),
             pltpu.SemaphoreType.DMA((120,)),
-            pltpu.SemaphoreType.DMA((9,)),
+            pltpu.SemaphoreType.DMA((5,)),
         ],
         compiler_params=pltpu.CompilerParams(
-            collective_id=0, has_side_effects=True, vmem_limit_bytes=56 * 1024 * 1024
+            collective_id=0, has_side_effects=True, vmem_limit_bytes=44 * 1024 * 1024
         ),
         cost_estimate=pl.CostEstimate(
             flops=12 * 512 * width * hid, bytes_accessed=8 * width * hid, transcendentals=0
         ),
-    )(tokens, up_weight, down_weight, grad_out, block_mask)
+    )(*[pltpu.with_memory_space_constraint(v, pltpu.HBM) for v in operands])
+    return pl.pallas_call(
+        write_out,
+        out_shape=[jax.ShapeDtypeStruct(shape, bf16) for shape in shapes],
+        in_specs=[anywhere] * 4,
+        out_specs=[anywhere] * 4,
+        scratch_shapes=[pltpu.SemaphoreType.DMA((4,))],
+        compiler_params=pltpu.CompilerParams(vmem_limit_bytes=1024 * 1024),
+    )(*results)
 
 
 def solution(mesh):

time: 83 us -> 66.3 us (0.80)
  local copies, waits for them, and re-layouts: 9.09 us -> 0 us
  Pallas kernels: 73 us -> 65.6 us
    unnamed x7 -> x0, local copies, waits for them, and re-layouts: 9.09 us -> none
    pallas_call x1 -> x2, Pallas kernels: 73 us -> 65.6 us  [the longest x1 63.3 us: layer(): pl.pallas_call(kernel, out_shape=[V(shape, bf16) for shape in shapes], in...]
where the time goes in v2:
time: 66.3 us; the launch traced here: 66.2 us
  Pallas kernels  65.6 us (99%)
    pallas_call x1, Pallas kernels, layer(): pl.pallas_call(kernel, out_shape=[V(shape, bf16) for shape in shapes], in...  63.3 us
    pallas_call x1, Pallas kernels, layer(): pl.pallas_call(write_out, out_shape=[jax.ShapeDtypeStruct(shape, bf16) fo...  2.25 us

profile of v2, /device:TPU:1, one launch (start us, length us, event | category | flops | bytes accessed | tf_op | source)
XLA Modules:
  0.0 66.2 jit_solution(2179402020996882422)
XLA Ops:
  0.6 63.3 %shard_map.84 = (bf16[16,1536]{1,0:T(8,128)(2,1)S(1)}, bf16[16,1536]{1,0:T(8,128)(2,1)S(1)}, bf16[1536,768]{1,0:T(8,128)(2,1)S(1)}, bf16[768,1536]{1,0:T(8,128)(2,1)S(1)}) custom-call(bf16[16,1536]{1,0:T(8,128)(2,1)} %tok_h.1, bf16[1536,768]{1,0:T(8,128)(2,1)} %up_h.1, bf16[768,1536]{1,0:T(8,128)(2,1)} %down_h.1, bf16[16,1536]{1,0:T(8,128)(2,1)} %gout_h.1, ...), custom_call_target="tpu_custom_call" | custom-call | flops 7247757312 | bytes 9437184 | tf_op jit(solution)/shard_map/pallas_call | solution.py:346
  64.0 2.3 %shard_map.85 = (bf16[16,1536]{1,0:T(8,128)(2,1)}, bf16[16,1536]{1,0:T(8,128)(2,1)}, bf16[1536,768]{1,0:T(8,128)(2,1)}, bf16[768,1536]{1,0:T(8,128)(2,1)}) custom-call(bf16[16,1536]{1,0:T(8,128)(2,1)S(1)} %get-tuple-element.8.refs_0_, bf16[16,1536]{1,0:T(8,128)(2,1)S(1)} %get-tuple-element.9.refs_1_, bf16[1536,768]{1,0:T(8,128)(2,1)S(1)} %get-tuple-element.10.refs_2_, ...), custom_call_target="tpu_custom_call" | custom-call | tf_op jit(solution)/shard_map/pallas_call | solution.py:387

commit v3 on v2

--- a/solution.py
+++ b/solution.py
@@ -7,18 +7,20 @@
 
 BLOCK = 256
 RING = 4
+SEMS = 192
 MESH = pl.DeviceIdType.MESH
 
 gelu_scale = 0.7978845608028654
 gelu_cubic = 0.044715
 
 SCHEDULE = (
-    "own0", "own1", "mm00", "mm10", "comb00", "comb10", "pass0", "pass1", "fin00", "mm03", "mm01",
-    "mm13", "last0", "last1", "comb03", "mm02", "mm12", "tt", "comb13", "fin03", "comb01",
-    "comb02", "comb12", "mm11", "agf03", "fin02", "fin01", "fin12", "comb11", "om03", "agf02",
-    "fin13", "agf12", "zs03", "fin11", "agf01", "om02", "agf13", "fin10", "om12", "agf11", "zs02",
-    "om01", "zs12", "om13", "om11", "agf00", "zs01", "agf10", "zs13", "zc0", "zs11", "zc1", "om00",
-    "om10", "at", "gup0", "zs00", "gup1", "gup2", "zs10", "zf0", "zf1", "gdn", "yf0", "yf1",
+    "own0", "own1", "far1", "far0", "mm00", "mm10", "pass0", "pass1", "comb00", "mm03", "mm01",
+    "mm11", "mm13", "last0", "last1", "comb03", "mm02", "mm12", "comb01", "comb11", "tt", "comb13",
+    "comb02", "fin00", "comb12", "fin03", "fin02", "fin01", "fin12", "fin11", "agf02", "fin13",
+    "agf12", "comb10", "agf11", "agf03", "agf01", "om02", "agf13", "agf00", "om12", "fin10",
+    "zs02", "om11", "om03", "zs12", "om01", "om13", "om00", "zs03", "zs01", "zs11", "agf10",
+    "zs13", "zc00", "at", "zc01", "zs00", "zc10", "zc11", "om10", "gup1", "gup0", "zs10", "zf00",
+    "zf10", "gup2", "zf01", "zf11", "gdn", "yf0", "yf1",
 )
 
 
@@ -63,6 +65,7 @@
         return {"row": turn(x, by)}
 
     sibling = {"depth": other}
+    columns = (pl.ds(0, width // 2), pl.ds(width // 2, width // 2))
     numbers = {}
 
     def remote(name, src, dst, peer):
@@ -83,6 +86,12 @@
         remote(name, dst, dst, sibling).wait_recv()
 
     sources = (tok_h, gout_h)
+    peers = [row_peer(1), row_peer(3), sibling]
+    for by in (1, 2, 3):
+        peers += [minor_peer(0, by), minor_peer(1, by)]
+    barrier = pltpu.get_barrier_semaphore()
+    for peer in peers:
+        pl.semaphore_signal(barrier, inc=1, device_id=peer, device_id_type=MESH)
     loads = [
         pltpu.make_async_copy(sources[0], feats.at[0, z, y, d], local_sem.at[0]),
         pltpu.make_async_copy(sources[1], feats.at[1, y, z, d], local_sem.at[1]),
@@ -92,13 +101,6 @@
     ]
     for load in loads:
         load.start()
-
-    peers = [row_peer(1), row_peer(3), sibling]
-    for by in (1, 2, 3):
-        peers += [minor_peer(0, by), minor_peer(1, by)]
-    barrier = pltpu.get_barrier_semaphore()
-    for peer in peers:
-        pl.semaphore_signal(barrier, inc=1, device_id=peer, device_id_type=MESH)
     pl.semaphore_wait(barrier, len(peers))
 
     hidden_corner = (col * 2 + d) * (hid // BLOCK)
@@ -107,9 +109,19 @@
     def mask_at(which, hb, fb):
         return masks[which, feature_corner + fb, hidden_corner + hb].astype(f32)
 
+    def here(s, a, m, count=None):
+        place = m if count is None else pl.ds(m, count)
+        return feats.at[s, a, place, d]
+
     for s in (0, 1):
         for by in (1, 3, 2):
-            send(("g1", s, by), sources[s], feats.at[s, major[s], minor[s], d], minor_peer(s, by))
+            send(("g1", s, by), sources[s], here(s, major[s], minor[s]), minor_peer(s, by))
+    for s in (0, 1):
+        mine = here(s, major[s], minor[s])
+        for by in (1, 3):
+            send(("g2", s, by, 0), sources[s], mine, major_peer(s, by))
+        send(("pair", s, 0, 0), sources[s], mine, sibling)
+
     loads[3].wait()
     loads[2].wait()
     for fb in range(width // BLOCK):
@@ -121,27 +133,39 @@
         for hb in range(hid // BLOCK):
             tile = (pl.ds(hb * BLOCK, BLOCK), pl.ds(fb * BLOCK, BLOCK))
             wd[tile] = wd[tile] * mask_at(1, hb, fb).astype(bf16)
+    def pass_on(s, steps):
+        for step in steps:
+            m = turn(minor[s], RING - step)
+            block = here(s, major[s], m)
+            arrived(("g1", s, step), block)
+            for by in (1, 3):
+                send(("g2", s, by, step), block, block, major_peer(s, by))
+            send(("pair", s, 0, step), block, block, sibling)
+
     def do_own(s):
+        pass_on(s, (1, 3))
+
+    def do_far(s):
+        pass_on(s, (2,))
         loads[s].wait()
-        for by in (1, 3, 2):
-            arrived(("g1", s, by), feats.at[s, major[s], turn(minor[s], RING - by), d])
-        mine = feats.at[s, major[s], :, d]
-        send(("g2", s, 1), mine, mine, major_peer(s, 1))
-        send(("g2", s, 3), mine, mine, major_peer(s, 3))
-        send(("pair", s, 0), mine, mine, sibling)
+
     def do_pass(s):
+        for step in (0, 1, 3, 2):
+            for by in (1, 3):
+                m = turn(minor[s], RING - step)
+                block = here(s, turn(major[s], RING - by), m)
+                arrived(("g2", s, by, step), block)
         for by, half in ((1, 0), (3, 2)):
             a = turn(major[s], RING - by)
-            whole = feats.at[s, a, :, d]
-            arrived(("g2", s, by), whole)
-            part_of = feats.at[s, a, pl.ds(half, 2), d]
+            part_of = here(s, a, half, 2)
             send(("g3", s, by), part_of, part_of, major_peer(s, by))
+            whole = here(s, a, 0, RING)
             send(("pair", s, RING - by), whole, whole, sibling)
 
     def do_last(s):
         a = turn(major[s], 2)
         for by, half in ((1, 0), (3, 2)):
-            part_of = feats.at[s, a, pl.ds(half, 2), d]
+            part_of = here(s, a, half, 2)
             arrived(("g3", s, by), part_of)
             send(("pair2", s, by), part_of, part_of, sibling)
 
@@ -168,6 +192,10 @@
         if k == 2:
             for by, half in ((1, 0), (3, 2)):
                 arrived(("pair2", s, by), feats.at[s, a, pl.ds(half, 2), other])
+        elif k == 0:
+            for step in range(RING):
+                block = feats.at[s, a, turn(minor[s], RING - step), other]
+                arrived(("pair", s, 0, step), block)
         else:
             arrived(("pair", s, k), feats.at[s, a, :, other])
         left = jnp.concatenate(
@@ -237,40 +265,50 @@
             kept[s, k] = total
             return
         zsend[s, k] = total.astype(bf16)
-        first, second = zsend.at[s, k, pl.ds(0, 2)], zsend.at[s, k, pl.ds(2, 2)]
-        if k == 2:
-            send(("z1", s, 1), first, zrelay.at[s, 0], major_peer(s, 1))
-            send(("z1", s, 3), second, zrelay.at[s, 1], major_peer(s, 3))
-        elif k == 1:
-            send(("z0", s, 1), second, zown.at[s, 0], major_peer(s, 1))
-        else:
-            send(("z0", s, 3), first, zown.at[s, 1], major_peer(s, 3))
-
-    def do_zc(s):
+        for h in (0, 1):
+            first, second = zsend.at[s, k, pl.ds(0, 2), :, columns[h]], zsend.at[s, k, pl.ds(2, 2), :, columns[h]]
+            if k == 2:
+                send(("z1", s, 1, h), first, zrelay.at[s, 0, :, :, columns[h]], major_peer(s, 1))
+                send(("z1", s, 3, h), second, zrelay.at[s, 1, :, :, columns[h]], major_peer(s, 3))
+            elif k == 1:
+                send(("z0", s, 1, h), second, zown.at[s, 0, :, :, columns[h]], major_peer(s, 1))
+            else:
+                send(("z0", s, 3, h), first, zown.at[s, 1, :, :, columns[h]], major_peer(s, 3))
+
+    def do_zc(s, h):
         for by, side, half in ((1, 0, 0), (3, 1, 2)):
-            arrived(("z1", s, by), zrelay.at[s, side])
-            total = zsend[s, by, pl.ds(half, 2)].astype(f32) + zrelay[s, side].astype(f32)
-            zcomb_out[s, side] = total.astype(bf16)
-            send(("z2", s, by), zcomb_out.at[s, side], zcomb_in.at[s, side], major_peer(s, by))
-
-    def do_zf(s):
+            where = (s, side, slice(None), slice(None), columns[h])
+            arrived(("z1", s, by, h), zrelay.at[where])
+            total = zsend[s, by, pl.ds(half, 2), :, columns[h]].astype(f32) + zrelay[where].astype(f32)
+            zcomb_out[where] = total.astype(bf16)
+            send(("z2", s, by, h), zcomb_out.at[where], zcomb_in.at[where], major_peer(s, by))
+
+    def do_zf(s, h):
+        cols = columns[h]
         for by, side in ((1, 0), (3, 1)):
-            arrived(("z0", s, by), zown.at[s, side])
-            arrived(("z2", s, by), zcomb_in.at[s, side])
+            arrived(("z0", s, by, h), zown.at[s, side, :, :, cols])
+            arrived(("z2", s, by, h), zcomb_in.at[s, side, :, :, cols])
+        for g in (0, 1):
+            rows = pl.ds(2 * g, 2)
+            total = (
+                kept[s, 0, rows, :, cols]
+                + zown[s, 1 - g, :, :, cols].astype(f32)
+                + zcomb_in[s, g, :, :, cols].astype(f32)
+            )
+            fsend[s, rows, :, cols] = total.astype(bf16)
+            fown[s, rows, :, cols] = total
+        for by in (1, 3, 2):
+            block = fsend.at[s, turn(minor[s], by), :, cols]
+            send(("f", s, by, h), block, frecv.at[s, by - 1, :, cols], minor_peer(s, by))
+
+    def do_yf(s):
         for h in (0, 1):
-            rows = pl.ds(2 * h, 2)
-            total = kept[s, 0, rows] + zown[s, 1 - h].astype(f32) + zcomb_in[s, h].astype(f32)
-            fsend[s, rows] = total.astype(bf16)
-            fown[s, rows] = total
-        for by in (1, 3, 2):
-            send(("f", s, by), fsend.at[s, turn(minor[s], by)], frecv.at[s, by - 1], minor_peer(s, by))
-
-    def do_yf(s):
-        total = fown[s, minor[s]]
-        for by in (1, 3, 2):
-            arrived(("f", s, by), frecv.at[s, by - 1])
-            total = total + frecv[s, by - 1].astype(f32)
-        (out_v, gtok_v)[s][...] = total.astype(bf16)
+            cols = columns[h]
+            total = fown[s, minor[s], :, cols]
+            for by in (1, 3, 2):
+                arrived(("f", s, by, h), frecv.at[s, by - 1, :, cols])
+                total = total + frecv[s, by - 1, :, cols].astype(f32)
+            (out_v, gtok_v)[s][:, cols] = total.astype(bf16)
 
     def do_tt():
         for a in range(RING):
@@ -314,7 +352,7 @@
                 ).astype(bf16)
 
     steps = {
-        "own": do_own, "pass": do_pass, "last": do_last, "mm": do_mm, "comb": do_comb, "fin": do_fin, "agf": do_agf,
+        "own": do_own, "far": do_far, "pass": do_pass, "last": do_last, "mm": do_mm, "comb": do_comb, "fin": do_fin, "agf": do_agf,
         "om": do_om, "zs": do_zs, "zc": do_zc, "zf": do_zf, "yf": do_yf,
         "tt": do_tt, "at": do_at, "gdn": do_gdn, "gup": do_gup,
     }
@@ -373,8 +411,8 @@
             V((2, 3, 16, width), bf16),
             V((width, 512), bf16),
             V((hid, 512), bf16),
-            pltpu.SemaphoreType.DMA((120,)),
-            pltpu.SemaphoreType.DMA((120,)),
+            pltpu.SemaphoreType.DMA((SEMS,)),
+            pltpu.SemaphoreType.DMA((SEMS,)),
             pltpu.SemaphoreType.DMA((5,)),
         ],
         compiler_params=pltpu.CompilerParams(

time: 66.3 us -> 62.5 us (0.943)
  Pallas kernels: 65.6 us -> 61.8 us
    pallas_call x1, Pallas kernels: 63.3 us -> 59.5 us  [layer(): pl.pallas_call(kernel, out_shape=[V(shape, bf16) for shape in shapes], in...]
where the time goes in v3:
time: 62.5 us; the launch traced here: 62.4 us
  Pallas kernels  61.8 us (99%)
  between operations  0.64 us (1%)
    pallas_call x1, Pallas kernels, layer(): pl.pallas_call(kernel, out_shape=[V(shape, bf16) for shape in shapes], in...  59.5 us
    pallas_call x1, Pallas kernels, layer(): pl.pallas_call(write_out, out_shape=[jax.ShapeDtypeStruct(shape, bf16) fo...  2.25 us

profile of v3, /device:TPU:1, one launch (start us, length us, event | category | flops | bytes accessed | tf_op | source)
XLA Modules:
  0.0 62.4 jit_solution(17131878346707409566)
XLA Ops:
  0.6 59.5 %shard_map.84 = (bf16[16,1536]{1,0:T(8,128)(2,1)S(1)}, bf16[16,1536]{1,0:T(8,128)(2,1)S(1)}, bf16[1536,768]{1,0:T(8,128)(2,1)S(1)}, bf16[768,1536]{1,0:T(8,128)(2,1)S(1)}) custom-call(bf16[16,1536]{1,0:T(8,128)(2,1)} %tok_h.1, bf16[1536,768]{1,0:T(8,128)(2,1)} %up_h.1, bf16[768,1536]{1,0:T(8,128)(2,1)} %down_h.1, bf16[16,1536]{1,0:T(8,128)(2,1)} %gout_h.1, ...), custom_call_target="tpu_custom_call" | custom-call | flops 7247757312 | bytes 9437184 | tf_op jit(solution)/shard_map/pallas_call | solution.py:384
  60.1 2.3 %shard_map.85 = (bf16[16,1536]{1,0:T(8,128)(2,1)}, bf16[16,1536]{1,0:T(8,128)(2,1)}, bf16[1536,768]{1,0:T(8,128)(2,1)}, bf16[768,1536]{1,0:T(8,128)(2,1)}) custom-call(bf16[16,1536]{1,0:T(8,128)(2,1)S(1)} %get-tuple-element.8.refs_0_, bf16[16,1536]{1,0:T(8,128)(2,1)S(1)} %get-tuple-element.9.refs_1_, bf16[1536,768]{1,0:T(8,128)(2,1)S(1)} %get-tuple-element.10.refs_2_, ...), custom_call_target="tpu_custom_call" | custom-call | tf_op jit(solution)/shard_map/pallas_call | solution.py:425

commit v4 on v3

--- a/solution.py
+++ b/solution.py
@@ -8,19 +8,21 @@
 BLOCK = 256
 RING = 4
 SEMS = 192
+DIRECT_SUMS = ((0, 0), (1, 0))
+DIRECT = ((1, 0), (1, 2))
 MESH = pl.DeviceIdType.MESH
 
 gelu_scale = 0.7978845608028654
 gelu_cubic = 0.044715
 
 SCHEDULE = (
-    "own0", "own1", "far1", "far0", "mm00", "mm10", "pass0", "pass1", "comb00", "mm03", "mm01",
-    "mm11", "mm13", "last0", "last1", "comb03", "mm02", "mm12", "comb01", "comb11", "tt", "comb13",
-    "comb02", "fin00", "comb12", "fin03", "fin02", "fin01", "fin12", "fin11", "agf02", "fin13",
-    "agf12", "comb10", "agf11", "agf03", "agf01", "om02", "agf13", "agf00", "om12", "fin10",
-    "zs02", "om11", "om03", "zs12", "om01", "om13", "om00", "zs03", "zs01", "zs11", "agf10",
-    "zs13", "zc00", "at", "zc01", "zs00", "zc10", "zc11", "om10", "gup1", "gup0", "zs10", "zf00",
-    "zf10", "gup2", "zf01", "zf11", "gdn", "yf0", "yf1",
+    "mask0", "own0", "own1", "mask1", "far0", "far1", "mm00", "mm10", "early0", "pass0", "early1",
+    "mm01", "pass1", "mm03", "mm11", "last0", "mm13", "last1", "mm02", "tt", "fin00", "comb01",
+    "comb03", "mm12", "comb02", "comb13", "comb11", "fin01", "fin03", "fin02", "fin11", "comb12",
+    "fin13", "agf01", "agf11", "agf03", "agf02", "agf13", "fin12", "agf00", "om01", "om11", "zs01",
+    "fin10", "om02", "om03", "zs11", "om13", "zs02", "zs13", "om12", "om00", "zs03", "zs12",
+    "om10", "zs00", "yg11", "yg02", "gup2", "at", "zs10", "yg13", "gup0", "yg01", "yg03", "gup1",
+    "yg12", "yg00", "gdn", "yg10", "yf1", "yf0",
 )
 
 
@@ -38,8 +40,8 @@
     tok_h, up_h, down_h, gout_h, mask_h,
     out_v, gtok_v, gup_v, gdown_v,
     feats, wu, wd, masks, part, own_part, relay, comb_out, comb_in, slopes, hidden,
-    pair_out, pair_in, kept, zsend, zrelay, zown, zcomb_out, zcomb_in, fsend, fown, frecv,
-    tok_t, act_t,
+    pair_out, pair_in, kept, ysend, yrecv, fsend, fown, frecv,
+    straight, tok_t, act_t,
     send_sem, recv_sem, local_sem,
 ):
     f32, bf16 = jnp.float32, jnp.bfloat16
@@ -65,7 +67,6 @@
         return {"row": turn(x, by)}
 
     sibling = {"depth": other}
-    columns = (pl.ds(0, width // 2), pl.ds(width // 2, width // 2))
     numbers = {}
 
     def remote(name, src, dst, peer):
@@ -86,7 +87,7 @@
         remote(name, dst, dst, sibling).wait_recv()
 
     sources = (tok_h, gout_h)
-    peers = [row_peer(1), row_peer(3), sibling]
+    peers = [row_peer(1), row_peer(2), row_peer(3), sibling]
     for by in (1, 2, 3):
         peers += [minor_peer(0, by), minor_peer(1, by)]
     barrier = pltpu.get_barrier_semaphore()
@@ -99,8 +100,8 @@
         pltpu.make_async_copy(mask_h, masks, local_sem.at[4]),
         pltpu.make_async_copy(down_h, wd, local_sem.at[3]),
     ]
-    for load in loads:
-        load.start()
+    for n in (0, 1, 3):
+        loads[n].start()
     pl.semaphore_wait(barrier, len(peers))
 
     hidden_corner = (col * 2 + d) * (hid // BLOCK)
@@ -109,9 +110,8 @@
     def mask_at(which, hb, fb):
         return masks[which, feature_corner + fb, hidden_corner + hb].astype(f32)
 
-    def here(s, a, m, count=None):
-        place = m if count is None else pl.ds(m, count)
-        return feats.at[s, a, place, d]
+    def here(s, a, m):
+        return feats.at[s, a, m, d]
 
     for s in (0, 1):
         for by in (1, 3, 2):
@@ -122,17 +122,18 @@
             send(("g2", s, by, 0), sources[s], mine, major_peer(s, by))
         send(("pair", s, 0, 0), sources[s], mine, sibling)
 
+    loads[2].start()
+    loads[4].start()
     loads[3].wait()
-    loads[2].wait()
-    for fb in range(width // BLOCK):
-        for hb in range(hid // BLOCK):
-            tile = (pl.ds(fb * BLOCK, BLOCK), pl.ds(hb * BLOCK, BLOCK))
-            wu[tile] = wu[tile] * mask_at(0, hb, fb).astype(bf16)
-    loads[4].wait()
-    for fb in range(width // BLOCK):
-        for hb in range(hid // BLOCK):
-            tile = (pl.ds(hb * BLOCK, BLOCK), pl.ds(fb * BLOCK, BLOCK))
-            wd[tile] = wd[tile] * mask_at(1, hb, fb).astype(bf16)
+
+    def do_mask(which):
+        loads[(2, 4)[which]].wait()
+        for fb in range(width // BLOCK):
+            for hb in range(hid // BLOCK):
+                features, units = pl.ds(fb * BLOCK, BLOCK), pl.ds(hb * BLOCK, BLOCK)
+                held, tile = ((wu, (features, units)), (wd, (units, features)))[which]
+                held[tile] = held[tile] * mask_at(which, hb, fb).astype(bf16)
+
     def pass_on(s, steps):
         for step in steps:
             m = turn(minor[s], RING - step)
@@ -149,25 +150,27 @@
         pass_on(s, (2,))
         loads[s].wait()
 
+    def relay_planes(s, steps):
+        for step in steps:
+            for by in (1, 3):
+                block = here(s, turn(major[s], RING - by), turn(minor[s], RING - step))
+                arrived(("g2", s, by, step), block)
+                if (step < 2) == (by == 1):
+                    send(("g3", s, by, step), block, block, major_peer(s, by))
+                send(("pair", s, RING - by, step), block, block, sibling)
+
+    def do_early(s):
+        relay_planes(s, (0, 1, 3))
+
     def do_pass(s):
-        for step in (0, 1, 3, 2):
-            for by in (1, 3):
-                m = turn(minor[s], RING - step)
-                block = here(s, turn(major[s], RING - by), m)
-                arrived(("g2", s, by, step), block)
-        for by, half in ((1, 0), (3, 2)):
-            a = turn(major[s], RING - by)
-            part_of = here(s, a, half, 2)
-            send(("g3", s, by), part_of, part_of, major_peer(s, by))
-            whole = here(s, a, 0, RING)
-            send(("pair", s, RING - by), whole, whole, sibling)
+        relay_planes(s, (2,))
 
     def do_last(s):
-        a = turn(major[s], 2)
-        for by, half in ((1, 0), (3, 2)):
-            part_of = here(s, a, half, 2)
-            arrived(("g3", s, by), part_of)
-            send(("pair2", s, by), part_of, part_of, sibling)
+        for step in (0, 3, 1, 2):
+            by = 1 if step < 2 else 3
+            block = here(s, turn(major[s], 2), turn(minor[s], RING - step))
+            arrived(("g3", s, by, step), block)
+            send(("pair", s, 2, step), block, block, sibling)
 
     def places(s, k):
         a = turn(major[s], k)
@@ -189,15 +192,8 @@
 
     def do_mm(s, k):
         a, m = places(s, k)
-        if k == 2:
-            for by, half in ((1, 0), (3, 2)):
-                arrived(("pair2", s, by), feats.at[s, a, pl.ds(half, 2), other])
-        elif k == 0:
-            for step in range(RING):
-                block = feats.at[s, a, turn(minor[s], RING - step), other]
-                arrived(("pair", s, 0, step), block)
-        else:
-            arrived(("pair", s, k), feats.at[s, a, :, other])
+        for step in range(RING):
+            arrived(("pair", s, k, step), feats.at[s, a, turn(minor[s], RING - step), other])
         left = jnp.concatenate(
             [feats[s, a, turn(m, j)].reshape(32, width) for j in range(RING)], axis=0
         )
@@ -206,6 +202,11 @@
             value = product(s, left, tile)
             part[s, k, :, :, tile] = value.astype(bf16).reshape(8, 16, BLOCK)
             own_part[s, k, :, :, tile] = value[:32].reshape(2, 16, BLOCK)
+        if (s, k) in DIRECT_SUMS:
+            for by in (2, 1, 3):
+                block = part.at[s, k, pl.ds(2 * by, 2)]
+                send(("x1", s, k, by), block, straight.at[s, k, by - 1], row_peer(by))
+            return
         send(("x1", s, k, 1), part.at[s, k, pl.ds(3, 2)], relay.at[s, 0, k], row_peer(1))
         send(("x1", s, k, 3), part.at[s, k, pl.ds(5, 2)], relay.at[s, 1, k], row_peer(3))
 
@@ -218,14 +219,19 @@
 
     def do_fin(s, k):
         a, m = places(s, k)
-        for by, side in ((1, 0), (3, 1)):
-            arrived(("x2", s, k, by), comb_in.at[s, side, k])
+        if (s, k) in DIRECT_SUMS:
+            for by in (1, 3, 2):
+                arrived(("x1", s, k, by), straight.at[s, k, by - 1])
+        else:
+            for by, side in ((1, 0), (3, 1)):
+                arrived(("x2", s, k, by), comb_in.at[s, side, k])
         for h in (0, 1):
-            total = (
-                own_part[s, k, h]
-                + relay[s, 1 - h, k, 1 - h].astype(f32)
-                + comb_in[s, h, k].astype(f32)
-            )
+            total = own_part[s, k, h]
+            if (s, k) in DIRECT_SUMS:
+                for n in range(RING - 1):
+                    total = total + straight[s, k, n, h].astype(f32)
+            else:
+                total = total + relay[s, 1 - h, k, 1 - h].astype(f32) + comb_in[s, h, k].astype(f32)
             if s == 0:
                 value, slope = gelu_pair(total)
                 hidden[s, a, m, h] = value.astype(bf16)
@@ -233,7 +239,7 @@
             else:
                 hidden[s, a, m, h] = (total * slopes[m, h]).astype(bf16)
         block = hidden.at[s, a, m]
-        for by in (1, 3):
+        for by in (2, 1, 3) if (s, k) in DIRECT else (1, 3):
             send(("a1", s, k, by), block, block, row_peer(by))
 
     def do_agf(s, k):
@@ -246,11 +252,14 @@
 
     def do_om(s, k):
         a, m = places(s, k)
-        for by, h in ((1, 0), (3, 1)):
-            arrived(("a2", s, k, by), hidden.at[s, a, turn(m, 2), h])
-        left = jnp.concatenate(
-            [hidden[s, a, :, other].reshape(64, hid), hidden[s, a, :, d].reshape(64, hid)], axis=0
-        )
+        if (s, k) in DIRECT:
+            for by in (1, 3, 2):
+                arrived(("a1", s, k, by), hidden.at[s, a, turn(m, RING - by)])
+        else:
+            for by, h in ((1, 0), (3, 1)):
+                arrived(("a2", s, k, by), hidden.at[s, a, turn(m, 2), h])
+        places_on = [turn(minor[s], j) for j in range(RING)]
+        left = jnp.concatenate([hidden[s, a, m, h] for h in (other, d) for m in places_on], axis=0)
         for n in range(width // BLOCK):
             tile = pl.ds(n * BLOCK, BLOCK)
             value = product_back(s, left, tile)
@@ -261,54 +270,28 @@
     def do_zs(s, k):
         arrived(("p", s, k), pair_in.at[s, k])
         total = kept[s, k] + pair_in[s, k].astype(f32)
+        kept[s, k, 0] = total[0]
+        ysend[s, k] = total[1:].astype(bf16)
+        for by in (2, 1, 3):
+            send(("y", s, k, by), ysend.at[s, k, by - 1], yrecv.at[s, k, by - 1], minor_peer(s, by))
+
+    def do_yg(s, k):
+        total = kept[s, k, 0]
+        for by in (1, 3, 2):
+            arrived(("y", s, k, by), yrecv.at[s, k, by - 1])
+            total = total + yrecv[s, k, by - 1].astype(f32)
         if k == 0:
-            kept[s, k] = total
-            return
-        zsend[s, k] = total.astype(bf16)
-        for h in (0, 1):
-            first, second = zsend.at[s, k, pl.ds(0, 2), :, columns[h]], zsend.at[s, k, pl.ds(2, 2), :, columns[h]]
-            if k == 2:
-                send(("z1", s, 1, h), first, zrelay.at[s, 0, :, :, columns[h]], major_peer(s, 1))
-                send(("z1", s, 3, h), second, zrelay.at[s, 1, :, :, columns[h]], major_peer(s, 3))
-            elif k == 1:
-                send(("z0", s, 1, h), second, zown.at[s, 0, :, :, columns[h]], major_peer(s, 1))
-            else:
-                send(("z0", s, 3, h), first, zown.at[s, 1, :, :, columns[h]], major_peer(s, 3))
-
-    def do_zc(s, h):
-        for by, side, half in ((1, 0, 0), (3, 1, 2)):
-            where = (s, side, slice(None), slice(None), columns[h])
-            arrived(("z1", s, by, h), zrelay.at[where])
-            total = zsend[s, by, pl.ds(half, 2), :, columns[h]].astype(f32) + zrelay[where].astype(f32)
-            zcomb_out[where] = total.astype(bf16)
-            send(("z2", s, by, h), zcomb_out.at[where], zcomb_in.at[where], major_peer(s, by))
-
-    def do_zf(s, h):
-        cols = columns[h]
-        for by, side in ((1, 0), (3, 1)):
-            arrived(("z0", s, by, h), zown.at[s, side, :, :, cols])
-            arrived(("z2", s, by, h), zcomb_in.at[s, side, :, :, cols])
-        for g in (0, 1):
-            rows = pl.ds(2 * g, 2)
-            total = (
-                kept[s, 0, rows, :, cols]
-                + zown[s, 1 - g, :, :, cols].astype(f32)
-                + zcomb_in[s, g, :, :, cols].astype(f32)
-            )
-            fsend[s, rows, :, cols] = total.astype(bf16)
-            fown[s, rows, :, cols] = total
+            fown[s] = total
+        else:
+            fsend[s, k - 1] = total.astype(bf16)
+            send(("f", s, k), fsend.at[s, k - 1], frecv.at[s, k - 1], major_peer(s, k))
+
+    def do_yf(s):
+        total = fown[s]
         for by in (1, 3, 2):
-            block = fsend.at[s, turn(minor[s], by), :, cols]
-            send(("f", s, by, h), block, frecv.at[s, by - 1, :, cols], minor_peer(s, by))
-
-    def do_yf(s):
-        for h in (0, 1):
-            cols = columns[h]
-            total = fown[s, minor[s], :, cols]
-            for by in (1, 3, 2):
-                arrived(("f", s, by, h), frecv.at[s, by - 1, :, cols])
-                total = total + frecv[s, by - 1, :, cols].astype(f32)
-            (out_v, gtok_v)[s][:, cols] = total.astype(bf16)
+            arrived(("f", s, by), frecv.at[s, by - 1])
+            total = total + frecv[s, by - 1].astype(f32)
+        (out_v, gtok_v)[s][...] = total.astype(bf16)
 
     def do_tt():
         for a in range(RING):
@@ -352,8 +335,8 @@
                 ).astype(bf16)
 
     steps = {
-        "own": do_own, "far": do_far, "pass": do_pass, "last": do_last, "mm": do_mm, "comb": do_comb, "fin": do_fin, "agf": do_agf,
-        "om": do_om, "zs": do_zs, "zc": do_zc, "zf": do_zf, "yf": do_yf,
+        "mask": do_mask, "own": do_own, "far": do_far, "early": do_early, "pass": do_pass, "last": do_last, "mm": do_mm, "comb": do_comb, "fin": do_fin, "agf": do_agf,
+        "om": do_om, "zs": do_zs, "yg": do_yg, "yf": do_yf,
         "tt": do_tt, "at": do_at, "gdn": do_gdn, "gup": do_gup,
     }
     for step in SCHEDULE:
@@ -401,14 +384,12 @@
             V((2, 4, 4, 16, width), bf16),
             V((2, 4, 4, 16, width), bf16),
             V((2, 4, 4, 16, width), f32),
-            V((2, 4, 4, 16, width), bf16),
-            V((2, 2, 2, 16, width), bf16),
-            V((2, 2, 2, 16, width), bf16),
-            V((2, 2, 2, 16, width), bf16),
-            V((2, 2, 2, 16, width), bf16),
-            V((2, 4, 16, width), bf16),
-            V((2, 4, 16, width), f32),
+            V((2, 4, 3, 16, width), bf16),
+            V((2, 4, 3, 16, width), bf16),
             V((2, 3, 16, width), bf16),
+            V((2, 16, width), f32),
+            V((2, 3, 16, width), bf16),
+            V((2, 4, 3, 2, 16, hid), bf16),
             V((width, 512), bf16),
             V((hid, 512), bf16),
             pltpu.SemaphoreType.DMA((SEMS,)),

time: 62.5 us -> 61.1 us (0.978)
  Pallas kernels: 61.8 us -> 60.4 us
    pallas_call x1, Pallas kernels: 59.5 us -> 58.1 us  [layer(): pl.pallas_call(kernel, out_shape=[V(shape, bf16) for shape in shapes], in...]
where the time goes in v4:
time: 61.1 us; the launch traced here: 61 us
  Pallas kernels  60.4 us (99%)
  between operations  0.64 us (1%)
    pallas_call x1, Pallas kernels, layer(): pl.pallas_call(kernel, out_shape=[V(shape, bf16) for shape in shapes], in...  58.1 us
    pallas_call x1, Pallas kernels, layer(): pl.pallas_call(write_out, out_shape=[jax.ShapeDtypeStruct(shape, bf16) fo...  2.25 us

profile of v4, /device:TPU:1, one launch (start us, length us, event | category | flops | bytes accessed | tf_op | source)
XLA Modules:
  0.0 61.0 jit_solution(11712997409776251287)
XLA Ops:
  0.6 58.1 %shard_map.84 = (bf16[16,1536]{1,0:T(8,128)(2,1)S(1)}, bf16[16,1536]{1,0:T(8,128)(2,1)S(1)}, bf16[1536,768]{1,0:T(8,128)(2,1)S(1)}, bf16[768,1536]{1,0:T(8,128)(2,1)S(1)}) custom-call(bf16[16,1536]{1,0:T(8,128)(2,1)} %tok_h.1, bf16[1536,768]{1,0:T(8,128)(2,1)} %up_h.1, bf16[768,1536]{1,0:T(8,128)(2,1)} %down_h.1, bf16[16,1536]{1,0:T(8,128)(2,1)} %gout_h.1, ...), custom_call_target="tpu_custom_call" | custom-call | flops 7247757312 | bytes 9437184 | tf_op jit(solution)/shard_map/pallas_call | solution.py:367
  58.7 2.3 %shard_map.85 = (bf16[16,1536]{1,0:T(8,128)(2,1)}, bf16[16,1536]{1,0:T(8,128)(2,1)}, bf16[1536,768]{1,0:T(8,128)(2,1)}, bf16[768,1536]{1,0:T(8,128)(2,1)}) custom-call(bf16[16,1536]{1,0:T(8,128)(2,1)S(1)} %get-tuple-element.8.refs_0_, bf16[16,1536]{1,0:T(8,128)(2,1)S(1)} %get-tuple-element.9.refs_1_, bf16[1536,768]{1,0:T(8,128)(2,1)S(1)} %get-tuple-element.10.refs_2_, ...), custom_call_target="tpu_custom_call" | custom-call | tf_op jit(solution)/shard_map/pallas_call | solution.py:406

commit v5 on v4

--- a/solution.py
+++ b/solution.py
@@ -21,8 +21,8 @@
     "comb03", "mm12", "comb02", "comb13", "comb11", "fin01", "fin03", "fin02", "fin11", "comb12",
     "fin13", "agf01", "agf11", "agf03", "agf02", "agf13", "fin12", "agf00", "om01", "om11", "zs01",
     "fin10", "om02", "om03", "zs11", "om13", "zs02", "zs13", "om12", "om00", "zs03", "zs12",
-    "om10", "zs00", "yg11", "yg02", "gup2", "at", "zs10", "yg13", "gup0", "yg01", "yg03", "gup1",
-    "yg12", "yg00", "gdn", "yg10", "yf1", "yf0",
+    "om10", "zs00", "zs10", "yg11", "yg02", "yg13", "at", "gup2", "yg01", "yg12", "yg03", "gup0",
+    "yg00", "gup1", "gdn", "yg10", "yf1", "yf0",
 )
 
 

time: 61.1 us -> 61.3 us (level)
  no operation moved by 1% of the time
where the time goes in v5:
time: 61.3 us; the launch traced here: 61.2 us
  Pallas kernels  60.5 us (99%)
  between operations  0.64 us (1%)
    pallas_call x1, Pallas kernels, layer(): pl.pallas_call(kernel, out_shape=[V(shape, bf16) for shape in shapes], in...  58.3 us
    pallas_call x1, Pallas kernels, layer(): pl.pallas_call(write_out, out_shape=[jax.ShapeDtypeStruct(shape, bf16) fo...  2.25 us

profile of v5, /device:TPU:1, one launch (start us, length us, event | category | flops | bytes accessed | tf_op | source)
XLA Modules:
  0.0 61.2 jit_solution(3552949151387869350)
XLA Ops:
  0.6 58.3 %shard_map.84 = (bf16[16,1536]{1,0:T(8,128)(2,1)S(1)}, bf16[16,1536]{1,0:T(8,128)(2,1)S(1)}, bf16[1536,768]{1,0:T(8,128)(2,1)S(1)}, bf16[768,1536]{1,0:T(8,128)(2,1)S(1)}) custom-call(bf16[16,1536]{1,0:T(8,128)(2,1)} %tok_h.1, bf16[1536,768]{1,0:T(8,128)(2,1)} %up_h.1, bf16[768,1536]{1,0:T(8,128)(2,1)} %down_h.1, bf16[16,1536]{1,0:T(8,128)(2,1)} %gout_h.1, ...), custom_call_target="tpu_custom_call" | custom-call | flops 7247757312 | bytes 9437184 | tf_op jit(solution)/shard_map/pallas_call | solution.py:367
  58.9 2.3 %shard_map.85 = (bf16[16,1536]{1,0:T(8,128)(2,1)}, bf16[16,1536]{1,0:T(8,128)(2,1)}, bf16[1536,768]{1,0:T(8,128)(2,1)}, bf16[768,1536]{1,0:T(8,128)(2,1)}) custom-call(bf16[16,1536]{1,0:T(8,128)(2,1)S(1)} %get-tuple-element.8.refs_0_, bf16[16,1536]{1,0:T(8,128)(2,1)S(1)} %get-tuple-element.9.refs_1_, bf16[1536,768]{1,0:T(8,128)(2,1)S(1)} %get-tuple-element.10.refs_2_, ...), custom_call_target="tpu_custom_call" | custom-call | tf_op jit(solution)/shard_map/pallas_call | solution.py:406
